TPU v7x, 32 devices: a whole 2x2x4 slice. The times are simulated.
32 devices in a mesh: groups: 2 (over y), tm: 4 (over z), space: 4 (over x, core).
Axes of the slice: x: 2, y: 2, z: 4, core: 2. Of those that a mesh axis runs over, the one named last changes fastest.
Arguments:
- solution: float32 [8, 16, 128, 128], P(('groups', 'tm'), 'space'), parts along dimension 0, may hold values from -6 to 6
- residual: float32 [8, 16, 128, 128], P(('groups', 'tm'), 'space'), parts along dimension 0, may hold values from -6 to 6
- direction: float32 [8, 16, 128, 128], P(('groups', 'tm'), 'space'), parts along dimension 0, may hold values from -6 to 6
- capacity: float32 [32, 128, 128], P(('groups', 'space')), parts along dimension 0, may hold values from 0.5 to 8
Outputs:
- new_solution: float32 [8, 16, 128, 128], P(('groups', 'tm'), 'space'), parts along dimension 0
- new_residual: float32 [8, 16, 128, 128], P(('groups', 'tm'), 'space'), parts along dimension 0
- new_direction: float32 [8, 16, 128, 128], P(('groups', 'tm'), 'space'), parts along dimension 0
There are 2 independent parts, one for each index of `groups`. A program takes and returns all parts, laid end to end along the dimension named above; each array names one. Nothing has to cross between parts.
All inputs are finite; a program needn't handle non-finite values.
Results may differ from a plain program's by a relative error of at most 0.000038.
Values sent between devices are 32-bit elements; how exact they have to be, the bound alone decides.
A program may use at most 64 MiB of HBM per device.

v0:
```python
import jax
import jax.numpy as jnp
from jax import lax
from jax.sharding import PartitionSpec as P


def padded_2(x, sides, width):
    for axis, dim in sides:
        peers, length = (lax.axis_size(axis), x.shape[dim])
        up = [(i, (i + 1) % peers) for i in range(peers - 1)]
        down = [(j, i) for i, j in up]
        last = lax.slice_in_dim(x, length - width, length, axis=dim)
        leading = lax.slice_in_dim(x, 0, width, axis=dim)
        before = lax.ppermute(last, axis, up)
        after = lax.ppermute(leading, axis, down)
        x = jnp.concatenate([before, x, after], axis=dim)
    return x


def shifted(x, axis, by):
    peers = lax.axis_size(axis)
    pairs = [(i, i + by) for i in range(peers) if 0 <= i + by < peers]
    return lax.ppermute(x, axis, pairs)


def combine(values, padded, neighbor, capacity):
    outer = jnp.pad(padded, ((0, 0), (0, 0), (1, 1), (1, 1)))
    beside = outer[:, 2:, 1:-1, 1:-1] + outer[:, :-2, 1:-1, 1:-1]
    beside = beside + outer[:, 1:-1, 2:, 1:-1] + outer[:, 1:-1, :-2, 1:-1]
    beside = beside + outer[:, 1:-1, 1:-1, 2:] + outer[:, 1:-1, 1:-1, :-2]
    return (6.0 + capacity) * values - beside - capacity * neighbor


def local(solution, residual, direction, capacity):
    stacked = padded_2(jnp.stack([residual, direction]), (("space", 2),), 1)
    res_pad = stacked[0]
    dir_pad = stacked[1]
    following = jnp.concatenate([residual[1:], shifted(residual, "tm", -1)], axis=0)
    previous = jnp.concatenate([shifted(direction, "tm", 1), direction[:-1]], axis=0)
    gradient = combine(residual, res_pad, following, capacity)
    image_field = combine(direction, dir_pad, previous, capacity)
    grad_norm = lax.psum(jnp.sum(gradient * gradient), ("tm", "space"))
    image_norm = lax.psum(jnp.sum(image_field * image_field), ("tm", "space"))
    step_size = grad_norm / image_norm
    new_solution = solution + step_size * direction
    new_residual = residual - step_size * image_field
    new_pad = padded_2(new_residual, (("space", 1),), 1)
    new_next = jnp.concatenate([new_residual[1:], shifted(new_residual, "tm", -1)], axis=0)
    new_gradient = combine(new_residual, new_pad, new_next, capacity)
    new_norm = lax.psum(jnp.sum(new_gradient * new_gradient), ("tm", "space"))
    new_direction = new_gradient + new_norm / grad_norm * direction
    return (new_solution, new_residual, new_direction)


def solution(mesh):
    placed = (
        P(("groups", "tm"), "space", None, None),
        P(("groups", "tm"), "space", None, None),
        P(("groups", "tm"), "space", None, None),
        P(("groups", "space"), None, None),
    )
    return jax.shard_map(
        local,
        mesh=mesh,
        in_specs=placed,
        out_specs=(
            P(("groups", "tm"), "space", None, None),
            P(("groups", "tm"), "space", None, None),
            P(("groups", "tm"), "space", None, None),
        ),
        check_vma=False,
    )
```

profile of v0, /device:TPU:0, one launch (start us, length us, event | category | flops | bytes accessed | tf_op | source)
XLA Modules:
  0.0 95.6 jit_solution(17781436251700958058)
XLA Ops:
  0.6 0.0 copy-start
  0.6 0.0 copy-start.1
  0.7 1.0 %pad_maximum_fusion.4 = (f32[2,1,1,128,128]{4,3,2,1,0:T(8,128)S(1)}, f32[2,1,1,128,128]{4,3,2,1,0:T(8,128)S(1)}) fusion(f32[1,1,4,128,128]{4,3,2,1,0:T(8,128)} %bitcast.36, f32[1,1,4,128,128]{4,3,2,1,0:T(8,128)} %bitcast.34), kind=kLoop, calls=%fused_computation.57 | loop fusion | flops 65536 | bytes 786432 | tf_op jit(solution)/shard_map/slice | solution.py:12
  1.7 2.4 %collective-permute-start = (f32[2,1,1,128,128]{4,3,2,1,0:T(8,128)S(1)}, f32[2,1,1,128,128]{4,3,2,1,0:T(8,128)S(1)}, u32[]{:S(2)}, u32[]{:S(2)}) collective-permute-start(f32[2,1,1,128,128]{4,3,2,1,0:T(8,128)S(1)} %get-tuple-element.11), channel_id=1, source_target_pairs={{0,1},{1,2},{2,3},{4,5},{5,6},{6,7},{8,9},{9,10},{10,11},{12,13},{... | collective-permute-start | bytes 393224 | tf_op jit(solution)/shard_map/ppermute | solution.py:14
  4.0 1.3 %collective-permute-start.1 = (f32[2,1,1,128,128]{4,3,2,1,0:T(8,128)S(1)}, f32[2,1,1,128,128]{4,3,2,1,0:T(8,128)S(1)}, u32[]{:S(2)}, u32[]{:S(2)}) collective-permute-start(f32[2,1,1,128,128]{4,3,2,1,0:T(8,128)S(1)} %get-tuple-element.12), channel_id=1, source_target_pairs={{1,0},{2,1},{3,2},{5,4},{6,5},{7,6},{9,8},{10,9},{11,10},{13,12},{... | collective-permute-start | bytes 393224 | tf_op jit(solution)/shard_map/ppermute | solution.py:15
  5.3 0.0 copy-done
  5.3 1.3 %collective-permute-start.2 = (f32[1,4,128,128]{3,2,1,0:T(8,128)S(1)}, f32[1,4,128,128]{3,2,1,0:T(8,128)S(1)}, u32[]{:S(2)}, u32[]{:S(2)}) collective-permute-start(f32[1,4,128,128]{3,2,1,0:T(8,128)S(1)} %copy-done), channel_id=1, source_target_pairs={{4,0},{8,4},{12,8},{5,1},{9,5},{13,9},{6,2},{10,6},{14,10},{7,3},{... | collective-permute-start | bytes 786440 | tf_op jit(solution)/shard_map/ppermute | solution.py:23
  6.6 0.0 copy-done.1
  6.7 5.0 %collective-permute-start.3 = (f32[1,4,128,128]{3,2,1,0:T(8,128)S(1)}, f32[1,4,128,128]{3,2,1,0:T(8,128)S(1)}, u32[]{:S(2)}, u32[]{:S(2)}) collective-permute-start(f32[1,4,128,128]{3,2,1,0:T(8,128)S(1)} %copy-done.1), channel_id=1, source_target_pairs={{0,4},{4,8},{8,12},{1,5},{5,9},{9,13},{2,6},{6,10},{10,14},{3,7},{... | collective-permute-start | bytes 786440 | tf_op jit(solution)/shard_map/ppermute | solution.py:23
  11.6 0.0 collective-permute-done
  11.6 0.0 collective-permute-done.1
  11.6 0.1 pad_maximum_fusion
  11.7 0.0 copy-start.3
  11.7 0.1 slice_bitcast_fusion
  11.8 3.1 %collective-permute-done.2 = f32[1,4,128,128]{3,2,1,0:T(8,128)S(1)} collective-permute-done((f32[1,4,128,128]{3,2,1,0:T(8,128)S(1)}, f32[1,4,128,128]{3,2,1,0:T(8,128)S(1)}, u32[]{:S(2)}, u32[]{:S(2)}) %collective-permute-start.2) | collective-permute-done | bytes 262176 | tf_op jit(solution)/shard_map/ppermute | solution.py:23
  14.9 1.8 %collective-permute-done.3 = f32[1,4,128,128]{3,2,1,0:T(8,128)S(1)} collective-permute-done((f32[1,4,128,128]{3,2,1,0:T(8,128)S(1)}, f32[1,4,128,128]{3,2,1,0:T(8,128)S(1)}, u32[]{:S(2)}, u32[]{:S(2)}) %collective-permute-start.3) | collective-permute-done | bytes 262176 | tf_op jit(solution)/shard_map/ppermute | solution.py:23
  16.6 0.0 copy-done.3
  16.6 1.0 %multiply_reduce_fusion.1 = (f32[]{:T(128)}, f32[1,4,128,128]{3,2,1,0:T(8,128)S(1)}, f32[]{:T(128)}) fusion(f32[1,4,128,128]{3,2,1,0:T(8,128)S(1)} %collective-permute-done.3, f32[4,128,128]{2,1,0:T(8,128)S(1)} %copy-done.3, f32[1,6,128,128]{3,2,1,0:T(8,128)S(1)} %get-tuple-element.9, f32[1,4,128,128]{3,2,1,0:T(8,128)S(1)} %copy-done.1, ...), kind=kLoop, calls=%fused_computation.54 | loop fusion | flops 1507326 | bytes 3407880 | tf_op jit(solution)/shard_map/reduce_sum | solution.py:43
  17.7 35.0 %all-reduce.3 = (f32[]{:T(128)}, f32[]{:T(128)}) all-reduce(f32[]{:T(128)} %get-tuple-element.17, f32[]{:T(128)} %get-tuple-element.7), channel_id=1, replica_groups=mesh['groups'=2,'tm'=4,'space'=4] {'tm','space'}, use_global_device_ids=true, to_apply=%region_1.2 | all-reduce | flops 2 | bytes 16 | tf_op jit(solution)/shard_map/psum | solution.py:42
  54.0 0.0 copy-start.2
  54.0 1.3 %collective-permute-start.6 = (f32[1,4,128,128]{3,2,1,0:T(8,128)S(1)}, f32[1,4,128,128]{3,2,1,0:T(8,128)S(1)}, u32[]{:S(2)}, u32[]{:S(2)}) collective-permute-start(f32[1,4,128,128]{3,2,1,0:T(8,128)S(1)} %multiply_subtract_fusion), channel_id=1, source_target_pairs={{4,0},{8,4},{12,8},{5,1},{9,5},{13,9},{6,2},{10,6},{14,10},{7,3},{... | collective-permute-start | bytes 786440 | tf_op jit(solution)/shard_map/ppermute | solution.py:23
  55.3 1.3 %collective-permute-start.4 = (f32[1,1,128,128]{3,2,1,0:T(8,128)S(1)}, f32[1,1,128,128]{3,2,1,0:T(8,128)S(1)}, u32[]{:S(2)}, u32[]{:S(2)}) collective-permute-start(f32[1,1,128,128]{3,2,1,0:T(8,128)S(1)} %get-tuple-element.16), channel_id=1, source_target_pairs={{1,0},{2,1},{3,2},{5,4},{6,5},{7,6},{9,8},{10,9},{11,10},{13,12},{... | collective-permute-start | bytes 196616 | tf_op jit(solution)/shard_map/ppermute | solution.py:15
  56.6 3.0 %collective-permute-start.5 = (f32[1,1,128,128]{3,2,1,0:T(8,128)S(1)}, f32[1,1,128,128]{3,2,1,0:T(8,128)S(1)}, u32[]{:S(2)}, u32[]{:S(2)}) collective-permute-start(f32[1,1,128,128]{3,2,1,0:T(8,128)S(1)} %get-tuple-element.15), channel_id=1, source_target_pairs={{0,1},{1,2},{2,3},{4,5},{5,6},{6,7},{8,9},{9,10},{10,11},{12,13},{... | collective-permute-start | bytes 196616 | tf_op jit(solution)/shard_map/ppermute | solution.py:14
  59.7 0.0 collective-permute-done.4
  59.7 0.9 collective-permute-done.5
  60.6 0.3 select_maximum_fusion
  60.8 0.0 copy-start.4
  60.9 1.5 %collective-permute-done.6 = f32[1,4,128,128]{3,2,1,0:T(8,128)S(1)} collective-permute-done((f32[1,4,128,128]{3,2,1,0:T(8,128)S(1)}, f32[1,4,128,128]{3,2,1,0:T(8,128)S(1)}, u32[]{:S(2)}, u32[]{:S(2)}) %collective-permute-start.6) | collective-permute-done | bytes 262176 | tf_op jit(solution)/shard_map/ppermute | solution.py:23
  62.4 0.0 copy-done.2
  62.4 0.9 multiply_reduce_fusion
  63.3 30.1 %psum.23 = f32[]{:T(128)} all-reduce(f32[]{:T(128)} %get-tuple-element.5), channel_id=1, replica_groups=mesh['groups'=2,'tm'=4,'space'=4] {'tm','space'}, use_global_device_ids=true, to_apply=%region_5.6 | all-reduce | flops 1 | bytes 8 | tf_op jit(solution)/shard_map/psum | solution.py:50
  94.7 0.0 copy-done.4
  94.7 0.8 multiply_add_fusion
  (2 shorter events, 0.0 us)
Async XLA Ops:
  0.6 4.7 %copy-start = (f32[1,4,128,128]{3,2,1,0:T(8,128)S(1)}, f32[1,4,128,128]{3,2,1,0:T(8,128)}, u32[]{:S(2)}) copy-start(f32[1,4,128,128]{3,2,1,0:T(8,128)} %param.5) | copy-start | bytes 786436
  0.6 6.0 %copy-start.1 = (f32[1,4,128,128]{3,2,1,0:T(8,128)S(1)}, f32[1,4,128,128]{3,2,1,0:T(8,128)}, u32[]{:S(2)}) copy-start(f32[1,4,128,128]{3,2,1,0:T(8,128)} %param.6) | copy-start | bytes 786436
  1.7 10.0 %collective-permute-start = (f32[2,1,1,128,128]{4,3,2,1,0:T(8,128)S(1)}, f32[2,1,1,128,128]{4,3,2,1,0:T(8,128)S(1)}, u32[]{:S(2)}, u32[]{:S(2)}) collective-permute-start(f32[2,1,1,128,128]{4,3,2,1,0:T(8,128)S(1)} %get-tuple-element.11), channel_id=1, source_target_pairs={{0,1},{1,2},{2,3},{4,5},{5,6},{6,7},{8,9},{9,10},{10,11},{12,13},{... | collective-permute-start | bytes 393224 | tf_op jit(solution)/shard_map/ppermute | solution.py:14
  4.0 7.6 %collective-permute-start.1 = (f32[2,1,1,128,128]{4,3,2,1,0:T(8,128)S(1)}, f32[2,1,1,128,128]{4,3,2,1,0:T(8,128)S(1)}, u32[]{:S(2)}, u32[]{:S(2)}) collective-permute-start(f32[2,1,1,128,128]{4,3,2,1,0:T(8,128)S(1)} %get-tuple-element.12), channel_id=1, source_target_pairs={{1,0},{2,1},{3,2},{5,4},{6,5},{7,6},{9,8},{10,9},{11,10},{13,12},{... | collective-permute-start | bytes 393224 | tf_op jit(solution)/shard_map/ppermute | solution.py:15
  5.3 9.5 %collective-permute-start.2 = (f32[1,4,128,128]{3,2,1,0:T(8,128)S(1)}, f32[1,4,128,128]{3,2,1,0:T(8,128)S(1)}, u32[]{:S(2)}, u32[]{:S(2)}) collective-permute-start(f32[1,4,128,128]{3,2,1,0:T(8,128)S(1)} %copy-done), channel_id=1, source_target_pairs={{4,0},{8,4},{12,8},{5,1},{9,5},{13,9},{6,2},{10,6},{14,10},{7,3},{... | collective-permute-start | bytes 786440 | tf_op jit(solution)/shard_map/ppermute | solution.py:23
  6.7 10.0 %collective-permute-start.3 = (f32[1,4,128,128]{3,2,1,0:T(8,128)S(1)}, f32[1,4,128,128]{3,2,1,0:T(8,128)S(1)}, u32[]{:S(2)}, u32[]{:S(2)}) collective-permute-start(f32[1,4,128,128]{3,2,1,0:T(8,128)S(1)} %copy-done.1), channel_id=1, source_target_pairs={{0,4},{4,8},{8,12},{1,5},{5,9},{9,13},{2,6},{6,10},{10,14},{3,7},{... | collective-permute-start | bytes 786440 | tf_op jit(solution)/shard_map/ppermute | solution.py:23
  11.7 4.9 %copy-start.3 = (f32[4,128,128]{2,1,0:T(8,128)S(1)}, f32[4,128,128]{2,1,0:T(8,128)}, u32[]{:S(2)}) copy-start(f32[4,128,128]{2,1,0:T(8,128)} %param.7) | copy-start | bytes 786436
  54.0 8.4 %copy-start.2 = (f32[1,4,128,128]{3,2,1,0:T(8,128)}, f32[1,4,128,128]{3,2,1,0:T(8,128)S(1)}, u32[]{:S(2)}) copy-start(f32[1,4,128,128]{3,2,1,0:T(8,128)S(1)} %multiply_subtract_fusion) | copy-start | bytes 786436
  54.0 8.4 %collective-permute-start.6 = (f32[1,4,128,128]{3,2,1,0:T(8,128)S(1)}, f32[1,4,128,128]{3,2,1,0:T(8,128)S(1)}, u32[]{:S(2)}, u32[]{:S(2)}) collective-permute-start(f32[1,4,128,128]{3,2,1,0:T(8,128)S(1)} %multiply_subtract_fusion), channel_id=1, source_target_pairs={{4,0},{8,4},{12,8},{5,1},{9,5},{13,9},{6,2},{10,6},{14,10},{7,3},{... | collective-permute-start | bytes 786440 | tf_op jit(solution)/shard_map/ppermute | solution.py:23
  55.3 4.3 %collective-permute-start.4 = (f32[1,1,128,128]{3,2,1,0:T(8,128)S(1)}, f32[1,1,128,128]{3,2,1,0:T(8,128)S(1)}, u32[]{:S(2)}, u32[]{:S(2)}) collective-permute-start(f32[1,1,128,128]{3,2,1,0:T(8,128)S(1)} %get-tuple-element.16), channel_id=1, source_target_pairs={{1,0},{2,1},{3,2},{5,4},{6,5},{7,6},{9,8},{10,9},{11,10},{13,12},{... | collective-permute-start | bytes 196616 | tf_op jit(solution)/shard_map/ppermute | solution.py:15
  56.6 3.9 %collective-permute-start.5 = (f32[1,1,128,128]{3,2,1,0:T(8,128)S(1)}, f32[1,1,128,128]{3,2,1,0:T(8,128)S(1)}, u32[]{:S(2)}, u32[]{:S(2)}) collective-permute-start(f32[1,1,128,128]{3,2,1,0:T(8,128)S(1)} %get-tuple-element.15), channel_id=1, source_target_pairs={{0,1},{1,2},{2,3},{4,5},{5,6},{6,7},{8,9},{9,10},{10,11},{12,13},{... | collective-permute-start | bytes 196616 | tf_op jit(solution)/shard_map/ppermute | solution.py:14
  60.8 33.9 %copy-start.4 = (f32[1,4,128,128]{3,2,1,0:T(8,128)S(1)}, f32[1,4,128,128]{3,2,1,0:T(8,128)}, u32[]{:S(2)}) copy-start(f32[1,4,128,128]{3,2,1,0:T(8,128)} %param.4) | copy-start | bytes 786436
where the time goes:
time: 95.9 us; the launch traced here: 95.6 us
  blocking collectives  65.1 us (68%)
  starting transfers between devices  15.5 us (16%)
  waiting for transfers between devices  7.27 us (8%)
  other arithmetic  4.14 us (4%)
  between operations  3.49 us (4%)
    psum x1, blocking collectives, local(): grad_norm = lax.psum(jnp.sum(gradient * gradient), ('tm', 'space'))  35 us
    psum x1, blocking collectives, local(): new_norm = lax.psum(jnp.sum(new_gradient * new_gradient), ('tm', 'space'))  30.1 us
    ppermute x3, starting transfers between devices, shifted(): return lax.ppermute(x, axis, pairs)  7.54 us
    ppermute x3, waiting for transfers between devices, shifted(): return lax.ppermute(x, axis, pairs)  6.39 us
    ppermute x2, starting transfers between devices, padded_2(): before = lax.ppermute(last, axis, up)  5.4 us
    ppermute x2, starting transfers between devices, padded_2(): after = lax.ppermute(leading, axis, down)  2.58 us
  transfers between devices with their start and end apart: 7, of which 4 were waited for; matrix products, arithmetic and copies ran while one was open for 0% of the time, Pallas kernels for 0%

commit v1 on v0

v1 whole, which is shorter than its diff:
```python
import functools

import jax
import jax.numpy as jnp
from jax import lax
from jax.experimental import pallas as pl
from jax.experimental.pallas import tpu as pltpu
from jax.sharding import PartitionSpec as P

MESH = pl.DeviceIdType.MESH


def beside(v, up, down):
    nx, ny = v.shape
    row = lax.broadcasted_iota(jnp.int32, v.shape, 0)
    col = lax.broadcasted_iota(jnp.int32, v.shape, 1)
    total = up + down
    total = total + jnp.where(row == 0, 0.0, pltpu.roll(v, 1, 0))
    total = total + jnp.where(row == nx - 1, 0.0, pltpu.roll(v, nx - 1, 0))
    total = total + jnp.where(col == 0, 0.0, pltpu.roll(v, 1, 1))
    return total + jnp.where(col == ny - 1, 0.0, pltpu.roll(v, ny - 1, 1))


def spatial(ref, halo, capacity, k):
    last = ref.shape[0] - 1
    v = ref[k]
    up = ref[k - 1] if k > 0 else halo[0]
    down = ref[k + 1] if k < last else halo[1]
    return (6.0 + capacity) * v - beside(v, up, down)


def folded(x):
    return jnp.sum(x, axis=0, keepdims=True)


def exchange(
    T, S, r_in, d_in, c_in, a_out, g_out, w_out, coef,
    rv, dv, cv, rn, dp, an, zr, zd, za, av, gv, wv, stats,
    in_sem, out_sem, t_send, t_recv, z_send, z_recv, s_send, s_recv,
):
    L = rv.shape[0]
    N = T * S
    t, s = lax.axis_index("tm"), lax.axis_index("space")
    me = t * S + s
    earlier, later = t > 0, t < T - 1
    lower, upper = s > 0, s < S - 1

    loads = [
        pltpu.make_async_copy(src, dst, in_sem.at[i])
        for i, (src, dst) in enumerate(((d_in, dv), (r_in, rv), (c_in, cv)))
    ]
    for load in loads:
        load.start()

    def peer(o):
        other = lax.rem(me + o, N)
        return {"tm": lax.div(other, S), "space": lax.rem(other, S)}

    def each_peer(do):
        if N <= 16:
            for o in range(1, N):
                do(o)
        else:
            def body(o, carry):
                do(o)
                return carry
            lax.fori_loop(1, N, body, 0)

    barrier = pltpu.get_barrier_semaphore()
    each_peer(lambda o: pl.semaphore_signal(barrier, inc=1, device_id=peer(o), device_id_type=MESH))

    @pl.when(jnp.logical_not(earlier))
    def _():
        dp[...] = jnp.zeros_like(dp)

    @pl.when(jnp.logical_not(later))
    def _():
        rn[...] = jnp.zeros_like(rn)
        an[...] = jnp.zeros_like(an)

    @pl.when(jnp.logical_not(lower))
    def _():
        for z in (zr, zd, za):
            z[0] = jnp.zeros(z.shape[1:], z.dtype)

    @pl.when(jnp.logical_not(upper))
    def _():
        for z in (zr, zd, za):
            z[1] = jnp.zeros(z.shape[1:], z.dtype)

    pl.semaphore_wait(barrier, N - 1)

    def step_copy(i, src, dst, k, to):
        return pltpu.make_async_remote_copy(
            src_ref=src.at[k], dst_ref=dst.at[k], send_sem=t_send.at[i, k], recv_sem=t_recv.at[i, k],
            device_id={"tm": to}, device_id_type=MESH)

    def layer_copy(i, src, dst, up):
        return pltpu.make_async_remote_copy(
            src_ref=src.at[L - 1 if up else 0], dst_ref=dst.at[0 if up else 1],
            send_sem=z_send.at[i, 0 if up else 1], recv_sem=z_recv.at[i, 0 if up else 1],
            device_id={"space": s + 1 if up else s - 1}, device_id_type=MESH)

    d_step = [step_copy(0, d_in, dp, k, t + 1) for k in range(L)]
    r_step = [step_copy(1, r_in, rn, k, t - 1) for k in range(L)]
    a_step = [step_copy(2, av, an, k, t - 1) for k in range(L)]
    d_up, d_down = layer_copy(0, d_in, zd, True), layer_copy(0, d_in, zd, False)
    r_up, r_down = layer_copy(1, r_in, zr, True), layer_copy(1, r_in, zr, False)
    a_up, a_down = layer_copy(2, av, za, True), layer_copy(2, av, za, False)

    @pl.when(upper)
    def _():
        d_up.start()

    @pl.when(lower)
    def _():
        d_down.start()

    @pl.when(later)
    def _():
        for copy in d_step:
            copy.start()

    @pl.when(earlier)
    def _():
        for copy in r_step:
            copy.start()

    @pl.when(upper)
    def _():
        r_up.start()

    @pl.when(lower)
    def _():
        r_down.start()

    def arrive(when, copy):
        @pl.when(when)
        def _():
            copy.wait_recv()

    for load in loads:
        load.wait()
    arrive(lower, d_up)
    arrive(upper, d_down)
    aa = jnp.zeros((1, cv.shape[2]), jnp.float32)
    for k in range(L):
        part = spatial(dv, zd, cv[k], k)
        arrive(earlier, d_step[k])
        image = part - cv[k] * dp[k]
        av[k] = image
        aa = aa + folded(image * image)

        @pl.when(earlier)
        def _():
            a_step[k].start()

        if k == 0:
            @pl.when(lower)
            def _():
                a_down.start()
        if k == L - 1:
            @pl.when(upper)
            def _():
                a_up.start()
    write_a = pltpu.make_async_copy(av, a_out, out_sem.at[0])
    write_a.start()

    arrive(lower, r_up)
    arrive(upper, r_down)
    gg = jnp.zeros((1, cv.shape[2]), jnp.float32)
    for k in range(L):
        part = spatial(rv, zr, cv[k], k)
        arrive(later, r_step[k])
        gradient = part - cv[k] * rn[k]
        gv[k] = gradient
        gg = gg + folded(gradient * gradient)
    write_g = pltpu.make_async_copy(gv, g_out, out_sem.at[1])
    write_g.start()

    arrive(lower, a_up)
    arrive(upper, a_down)
    gw = jnp.zeros((1, cv.shape[2]), jnp.float32)
    ww = jnp.zeros((1, cv.shape[2]), jnp.float32)
    for k in range(L):
        wv[k] = spatial(av, za, cv[k], k)
    for k in range(L):
        arrive(later, a_step[k])
        change = wv[k] - cv[k] * an[k]
        wv[k] = change
        gw = gw + folded(gv[k] * change)
        ww = ww + folded(change * change)

    stats[me] = jnp.concatenate([gg, aa, gw, ww, gg, aa, gw, ww], axis=0)

    def stat_copy(o):
        return pltpu.make_async_remote_copy(
            src_ref=stats.at[me], dst_ref=stats.at[me], send_sem=s_send.at[o], recv_sem=s_recv.at[me],
            device_id=peer(o), device_id_type=MESH)

    def stat_wait(o):
        other = lax.rem(me + o, N)
        pltpu.make_async_remote_copy(
            src_ref=stats.at[other], dst_ref=stats.at[other], send_sem=s_send.at[o], recv_sem=s_recv.at[other],
            device_id=peer(o), device_id_type=MESH).wait_recv()

    each_peer(lambda o: stat_copy(o).start())
    write_w = pltpu.make_async_copy(wv, w_out, out_sem.at[2])
    write_w.start()
    each_peer(stat_wait)

    whole = jnp.sum(jnp.sum(stats[...], axis=0), axis=1, keepdims=True)
    whole = jnp.broadcast_to(whole, (8, coef.shape[1]))
    grad_norm, image_norm, cross, change_norm = (whole[i:i + 1] for i in range(4))
    step_size = grad_norm / image_norm
    new_norm = grad_norm + step_size * (step_size * change_norm - 2.0 * cross)
    ratio = new_norm / grad_norm
    coef[...] = jnp.concatenate([step_size, ratio] * 4, axis=0)

    def sent(when, *copies):
        @pl.when(when)
        def _():
            for copy in copies:
                copy.wait_send()

    sent(later, *d_step)
    sent(earlier, *r_step, *a_step)
    sent(upper, d_up, r_up, a_up)
    sent(lower, d_down, r_down, a_down)
    each_peer(lambda o: stat_copy(o).wait_send())
    for write in (write_a, write_g, write_w):
        write.wait()


def local(T, S, solution, residual, direction, capacity):
    L, X, Y = capacity.shape
    field = jax.ShapeDtypeStruct((L, X, Y), jnp.float32)
    whole = pltpu.VMEM((L, X, Y), jnp.float32)
    halo = pltpu.VMEM((2, X, Y), jnp.float32)
    image, gradient, change, coef = pl.pallas_call(
        functools.partial(exchange, T, S),
        out_shape=(field, field, field, jax.ShapeDtypeStruct((8, Y), jnp.float32)),
        in_specs=[pl.BlockSpec(memory_space=pl.ANY)] * 3,
        out_specs=(pl.BlockSpec(memory_space=pl.ANY),) * 3 + (pl.BlockSpec(memory_space=pltpu.VMEM),),
        scratch_shapes=[whole] * 6 + [halo] * 3 + [whole] * 3 + [
            pltpu.VMEM((T * S, 8, Y), jnp.float32),
            pltpu.SemaphoreType.DMA((3,)),
            pltpu.SemaphoreType.DMA((3,)),
            pltpu.SemaphoreType.DMA((3, L)),
            pltpu.SemaphoreType.DMA((3, L)),
            pltpu.SemaphoreType.DMA((3, 2)),
            pltpu.SemaphoreType.DMA((3, 2)),
            pltpu.SemaphoreType.DMA((T * S,)),
            pltpu.SemaphoreType.DMA((T * S,)),
        ],
        compiler_params=pltpu.CompilerParams(
            collective_id=0, has_side_effects=True, vmem_limit_bytes=16 * 1024 * 1024),
    )(residual[0], direction[0], capacity)
    step_size, ratio = coef[0, 0], coef[1, 0]
    new_solution = solution + step_size * direction
    new_residual = residual - step_size * image[None]
    new_direction = gradient[None] - step_size * change[None] + ratio * direction
    return new_solution, new_residual, new_direction


def solution(mesh):
    field = P(("groups", "tm"), "space", None, None)
    return jax.shard_map(
        functools.partial(local, mesh.shape["tm"], mesh.shape["space"]),
        mesh=mesh,
        in_specs=(field, field, field, P(("groups", "space"), None, None)),
        out_specs=(field, field, field),
        check_vma=False,
    )
```

time: 95.9 us -> 29.1 us (0.30)
  blocking collectives: 65.1 us -> 0 us
  Pallas kernels: 0 us -> 22.6 us
  starting transfers between devices: 15.5 us -> 0 us
  waiting for transfers between devices: 7.27 us -> 0 us
  local copies, waits for them, and re-layouts: 0.09 us -> 3.44 us
  between operations: 3.49 us -> 0.65 us
  other arithmetic: 4.14 us -> 2.17 us
    psum x2 -> x0, blocking collectives: 65.1 us -> none  [the longest x1 35 us: local(): grad_norm = lax.psum(jnp.sum(gradient * gradient), ('tm', 'space'))]
    pallas_call x0 -> x1, Pallas kernels: none -> 22.6 us  [local(): pl.pallas_call(functools.partial(exchange, T, S), out_shape=(field, field...]
    ppermute x7 -> x0, starting transfers between devices: 15.5 us -> none  [the longest x3 7.54 us: shifted(): return lax.ppermute(x, axis, pairs)]
    ppermute x7 -> x0, waiting for transfers between devices: 7.27 us -> none  [the longest x3 6.39 us: shifted(): return lax.ppermute(x, axis, pairs)]
    unnamed x10 -> x8, local copies, waits for them, and re-layouts: 0.03 us -> 2.85 us
    reduce_sum x2 -> x0, other arithmetic: 1.92 us -> none  [the longest x1 1.02 us: local(): image_norm = lax.psum(jnp.sum(image_field * image_field), ('tm', 'space'))]
    add x1, other arithmetic: 0.84 us -> 2.17 us  [local(): gradient[None] - step_size * change[None] + ratio * direction]
    slice x1 -> x0, other arithmetic: 1.01 us -> none  [padded_2(): last = lax.slice_in_dim(x, length - width, length, axis=dim)]
  transfers between devices with their start and end apart: 7 -> 0, of which waited for: 4 -> 0; matrix products, arithmetic and copies ran while one was open for 0% -> 0% of each run, Pallas kernels for 0% -> 0%
where the time goes in v1:
time: 29.1 us; the launch traced here: 28.8 us
  Pallas kernels  22.6 us (78%)
  local copies, waits for them, and re-layouts  3.44 us (12%)
  other arithmetic  2.17 us (7%)
  between operations  0.65 us (2%)
    pallas_call x1, Pallas kernels, local(): pl.pallas_call(functools.partial(exchange, T, S), out_shape=(field, field...  22.6 us
    unnamed x8, local copies, waits for them, and re-layouts  2.85 us
    add x1, other arithmetic, local(): gradient[None] - step_size * change[None] + ratio * direction  2.17 us
    slice x1, local copies, waits for them, and re-layouts, local(): step_size, ratio = (coef[0, 0], coef[1, 0])  0.6 us

profile of v1, /device:TPU:0, one launch (start us, length us, event | category | flops | bytes accessed | tf_op | source)
XLA Modules:
  0.0 28.8 jit_solution(18118643611311049801)
XLA Ops:
  0.6 0.0 copy-start
  0.6 0.9 %copy-done = f32[1,4,128,128]{3,2,1,0:T(8,128)S(1)} copy-done((f32[1,4,128,128]{3,2,1,0:T(8,128)S(1)}, f32[1,4,128,128]{3,2,1,0:T(8,128)}, u32[]{:S(2)}) %copy-start) | copy-done | bytes 262168
  1.6 0.0 copy-start.1
  1.6 0.9 %copy-done.1 = f32[1,4,128,128]{3,2,1,0:T(8,128)S(1)} copy-done((f32[1,4,128,128]{3,2,1,0:T(8,128)S(1)}, f32[1,4,128,128]{3,2,1,0:T(8,128)}, u32[]{:S(2)}) %copy-start.1) | copy-done | bytes 262168
  2.5 0.0 copy-start.2
  2.5 0.9 %copy-done.2 = f32[4,128,128]{2,1,0:T(8,128)S(1)} copy-done((f32[4,128,128]{2,1,0:T(8,128)S(1)}, f32[4,128,128]{2,1,0:T(8,128)}, u32[]{:S(2)}) %copy-start.2) | copy-done | bytes 262168
  3.5 0.0 copy-start.3
  3.5 22.6 %shard_map.67 = (f32[4,128,128]{2,1,0:T(8,128)S(1)}, f32[4,128,128]{2,1,0:T(8,128)S(1)}, f32[4,128,128]{2,1,0:T(8,128)S(1)}, f32[8,128]{1,0:T(8,128)S(1)}) custom-call(f32[4,128,128]{2,1,0:T(8,128)S(1)} %bitcast.9, f32[4,128,128]{2,1,0:T(8,128)S(1)} %bitcast.8, f32[4,128,128]{2,1,0:T(8,128)S(1)} %copy-done.2), custom_call_target="tpu_custom_call" | custom-call | tf_op jit(solution)/shard_map/pallas_call | solution.py:240
  26.1 0.6 %fusion = (f32[1,1]{1,0:T(1,128)}, f32[1,1]{1,0:T(1,128)}) fusion(f32[8,128]{1,0:T(8,128)S(1)} %get-tuple-element.7), kind=kLoop, calls=%fused_computation.3 | loop fusion | bytes 16 | tf_op jit(solution)/shard_map/slice | solution.py:259
  26.7 0.0 copy-done.3
  26.7 2.2 %bitcast_add_fusion = (f32[1,4,128,128]{3,2,1,0:T(8,128)}, f32[1,4,128,128]{3,2,1,0:T(8,128)}, f32[1,4,128,128]{3,2,1,0:T(8,128)}) fusion(f32[1,4,128,128]{3,2,1,0:T(8,128)S(1)} %copy-done, f32[4,128,128]{2,1,0:T(8,128)S(1)} %get-tuple-element.9, f32[4,128,128]{2,1,0:T(8,128)S(1)} %get-tuple-element.10, f32[]{:T(128)} %bitcast.5, f32[]{:T(128)} %bitcast.2, ...), kind=kLoop, calls=%fused_computation | loop fusion | flops 524288 | bytes 2359304 | tf_op jit(solution)/shard_map/add | solution.py:262
Async XLA Ops:
  0.6 1.0 %copy-start = (f32[1,4,128,128]{3,2,1,0:T(8,128)S(1)}, f32[1,4,128,128]{3,2,1,0:T(8,128)}, u32[]{:S(2)}) copy-start(f32[1,4,128,128]{3,2,1,0:T(8,128)} %param.6) | copy-start | bytes 786436
  1.6 0.9 %copy-start.1 = (f32[1,4,128,128]{3,2,1,0:T(8,128)S(1)}, f32[1,4,128,128]{3,2,1,0:T(8,128)}, u32[]{:S(2)}) copy-start(f32[1,4,128,128]{3,2,1,0:T(8,128)} %param.5) | copy-start | bytes 786436
  2.5 0.9 %copy-start.2 = (f32[4,128,128]{2,1,0:T(8,128)S(1)}, f32[4,128,128]{2,1,0:T(8,128)}, u32[]{:S(2)}) copy-start(f32[4,128,128]{2,1,0:T(8,128)} %c_in.1) | copy-start | bytes 786436
  3.5 23.2 %copy-start.3 = (f32[1,4,128,128]{3,2,1,0:T(8,128)S(1)}, f32[1,4,128,128]{3,2,1,0:T(8,128)}, u32[]{:S(2)}) copy-start(f32[1,4,128,128]{3,2,1,0:T(8,128)} %param.4) | copy-start | bytes 786436

commit v2 on v1

--- a/solution.py
+++ b/solution.py
@@ -34,9 +34,9 @@
 
 
 def exchange(
-    T, S, r_in, d_in, c_in, a_out, g_out, w_out, coef,
-    rv, dv, cv, rn, dp, an, zr, zd, za, av, gv, wv, stats,
-    in_sem, out_sem, t_send, t_recv, z_send, z_recv, s_send, s_recv,
+    T, S, x_in, r_in, d_in, c_in, xv, rv, dv, av, gv, wv, coef,
+    cv, rn, dp, an, zr, zd, za, stats,
+    in_sem, t_send, t_recv, z_send, z_recv, s_send, s_recv,
 ):
     L = rv.shape[0]
     N = T * S
@@ -47,7 +47,7 @@
 
     loads = [
         pltpu.make_async_copy(src, dst, in_sem.at[i])
-        for i, (src, dst) in enumerate(((d_in, dv), (r_in, rv), (c_in, cv)))
+        for i, (src, dst) in enumerate(((d_in, dv), (c_in, cv), (r_in, rv), (x_in, xv)))
     ]
     for load in loads:
         load.start()
@@ -163,8 +163,6 @@
             @pl.when(upper)
             def _():
                 a_up.start()
-    write_a = pltpu.make_async_copy(av, a_out, out_sem.at[0])
-    write_a.start()
 
     arrive(lower, r_up)
     arrive(upper, r_down)
@@ -175,8 +173,6 @@
         gradient = part - cv[k] * rn[k]
         gv[k] = gradient
         gg = gg + folded(gradient * gradient)
-    write_g = pltpu.make_async_copy(gv, g_out, out_sem.at[1])
-    write_g.start()
 
     arrive(lower, a_up)
     arrive(upper, a_down)
@@ -205,8 +201,6 @@
             device_id=peer(o), device_id_type=MESH).wait_recv()
 
     each_peer(lambda o: stat_copy(o).start())
-    write_w = pltpu.make_async_copy(wv, w_out, out_sem.at[2])
-    write_w.start()
     each_peer(stat_wait)
 
     whole = jnp.sum(jnp.sum(stats[...], axis=0), axis=1, keepdims=True)
@@ -228,7 +222,20 @@
     sent(upper, d_up, r_up, a_up)
     sent(lower, d_down, r_down, a_down)
     each_peer(lambda o: stat_copy(o).wait_send())
-    for write in (write_a, write_g, write_w):
+
+
+def finish(x, r, d, a, g, w, coef, x_out, r_out, d_out, xs, rs, ds, sem):
+    step_size, ratio = coef[0:1], coef[1:2]
+    writes = []
+    for k in range(x.shape[0]):
+        xs[k] = x[k] + step_size * d[k]
+        rs[k] = r[k] - step_size * a[k]
+        ds[k] = g[k] - step_size * w[k] + ratio * d[k]
+        for i, (src, dst) in enumerate(((xs, x_out), (rs, r_out), (ds, d_out))):
+            write = pltpu.make_async_copy(src.at[k], dst.at[k], sem.at[i, k])
+            write.start()
+            writes.append(write)
+    for write in writes:
         write.wait()
 
 
@@ -237,15 +244,15 @@
     field = jax.ShapeDtypeStruct((L, X, Y), jnp.float32)
     whole = pltpu.VMEM((L, X, Y), jnp.float32)
     halo = pltpu.VMEM((2, X, Y), jnp.float32)
-    image, gradient, change, coef = pl.pallas_call(
+    near, far = pl.BlockSpec(memory_space=pltpu.VMEM), pl.BlockSpec(memory_space=pltpu.HBM)
+    kept = pl.pallas_call(
         functools.partial(exchange, T, S),
-        out_shape=(field, field, field, jax.ShapeDtypeStruct((8, Y), jnp.float32)),
-        in_specs=[pl.BlockSpec(memory_space=pl.ANY)] * 3,
-        out_specs=(pl.BlockSpec(memory_space=pl.ANY),) * 3 + (pl.BlockSpec(memory_space=pltpu.VMEM),),
-        scratch_shapes=[whole] * 6 + [halo] * 3 + [whole] * 3 + [
+        out_shape=(field,) * 6 + (jax.ShapeDtypeStruct((8, Y), jnp.float32),),
+        in_specs=[far] * 4,
+        out_specs=(near,) * 7,
+        scratch_shapes=[whole] * 4 + [halo] * 3 + [
             pltpu.VMEM((T * S, 8, Y), jnp.float32),
-            pltpu.SemaphoreType.DMA((3,)),
-            pltpu.SemaphoreType.DMA((3,)),
+            pltpu.SemaphoreType.DMA((4,)),
             pltpu.SemaphoreType.DMA((3, L)),
             pltpu.SemaphoreType.DMA((3, L)),
             pltpu.SemaphoreType.DMA((3, 2)),
@@ -254,13 +261,17 @@
             pltpu.SemaphoreType.DMA((T * S,)),
         ],
         compiler_params=pltpu.CompilerParams(
-            collective_id=0, has_side_effects=True, vmem_limit_bytes=16 * 1024 * 1024),
-    )(residual[0], direction[0], capacity)
-    step_size, ratio = coef[0, 0], coef[1, 0]
-    new_solution = solution + step_size * direction
-    new_residual = residual - step_size * image[None]
-    new_direction = gradient[None] - step_size * change[None] + ratio * direction
-    return new_solution, new_residual, new_direction
+            collective_id=0, has_side_effects=True, vmem_limit_bytes=53568 * 1024),
+    )(solution[0], residual[0], direction[0], capacity)
+    outs = pl.pallas_call(
+        finish,
+        out_shape=(field,) * 3,
+        in_specs=[near] * 7,
+        out_specs=(far,) * 3,
+        scratch_shapes=[whole] * 3 + [pltpu.SemaphoreType.DMA((3, L))],
+        compiler_params=pltpu.CompilerParams(vmem_limit_bytes=16 * 1024 * 1024),
+    )(*kept)
+    return tuple(out[None] for out in outs)
 
 
 def solution(mesh):

time: 29.1 us -> 24.5 us (0.84)
  local copies, waits for them, and re-layouts: 3.44 us -> 0 us
  other arithmetic: 2.17 us -> 0 us
  Pallas kernels: 22.6 us -> 23.7 us
    unnamed x8 -> x0, local copies, waits for them, and re-layouts: 2.85 us -> none
    add x1 -> x0, other arithmetic: 2.17 us -> none  [local(): gradient[None] - step_size * change[None] + ratio * direction]
    pallas_call x1 -> x2, Pallas kernels: 22.6 us -> 23.7 us  [the longest x1 22.7 us: local(): pl.pallas_call(functools.partial(exchange, T, S), out_shape=(field,) * 6...]
    slice x1 -> x0, local copies, waits for them, and re-layouts: 0.6 us -> none  [local(): step_size, ratio = (coef[0, 0], coef[1, 0])]
where the time goes in v2:
time: 24.5 us; the launch traced here: 24.4 us
  Pallas kernels  23.7 us (97%)
  between operations  0.64 us (3%)
    pallas_call x1, Pallas kernels, local(): pl.pallas_call(functools.partial(exchange, T, S), out_shape=(field,) * 6...  22.7 us
    pallas_call x1, Pallas kernels, local(): pl.pallas_call(finish, out_shape=(field,) * 3, in_specs=[near] * 7, out_s...  0.98 us

profile of v2, /device:TPU:0, one launch (start us, length us, event | category | flops | bytes accessed | tf_op | source)
XLA Modules:
  0.0 24.4 jit_solution(1245693201335039121)
XLA Ops:
  0.6 22.7 %shard_map.67 = (f32[4,128,128]{2,1,0:T(8,128)S(1)}, f32[4,128,128]{2,1,0:T(8,128)S(1)}, f32[4,128,128]{2,1,0:T(8,128)S(1)}, f32[4,128,128]{2,1,0:T(8,128)S(1)},...) custom-call(f32[4,128,128]{2,1,0:T(8,128)} %bitcast.6, f32[4,128,128]{2,1,0:T(8,128)} %bitcast.7, ...), custom_call_target="tpu_custom_call" | custom-call | tf_op jit(solution)/shard_map/pallas_call | solution.py:248
  23.4 1.0 %shard_map.68 = (f32[4,128,128]{2,1,0:T(8,128)}, f32[4,128,128]{2,1,0:T(8,128)}, f32[4,128,128]{2,1,0:T(8,128)}) custom-call(f32[4,128,128]{2,1,0:T(8,128)S(1)} %get-tuple-element.13.x, f32[4,128,128]{2,1,0:T(8,128)S(1)} %get-tuple-element.14.r, f32[4,128,128]{2,1,0:T(8,128)S(1)} %get-tuple-element.15.d, f32[4,128,128]{2,1,0:T(8,128)S(1)} %get-tuple-element.16.a, ...), custom_call_target="tpu_custom_call" | custom-call | tf_op jit(solution)/shard_map/pallas_call | solution.py:266

commit v3 on v2

v3 whole, which is shorter than its diff:
```python
import functools

import jax
import jax.numpy as jnp
from jax import lax
from jax.experimental import pallas as pl
from jax.experimental.pallas import tpu as pltpu
from jax.sharding import PartitionSpec as P

MESH = pl.DeviceIdType.MESH


def beside(v, up, down):
    nx, ny = v.shape
    row = lax.broadcasted_iota(jnp.int32, v.shape, 0)
    col = lax.broadcasted_iota(jnp.int32, v.shape, 1)
    total = up + down
    total = total + jnp.where(row == 0, 0.0, pltpu.roll(v, 1, 0))
    total = total + jnp.where(row == nx - 1, 0.0, pltpu.roll(v, nx - 1, 0))
    total = total + jnp.where(col == 0, 0.0, pltpu.roll(v, 1, 1))
    return total + jnp.where(col == ny - 1, 0.0, pltpu.roll(v, ny - 1, 1))


def spatial(ref, halo, capacity, k):
    last = ref.shape[0] - 1
    v = ref[k]
    up = ref[k - 1] if k > 0 else halo[0]
    down = ref[k + 1] if k < last else halo[1]
    return (6.0 + capacity) * v - beside(v, up, down)


def folded(x):
    return jnp.sum(x, axis=0, keepdims=True)


def exchange(
    T, S, x_in, r_in, d_in, c_in, xv, rv, dv, av, gv, wv, coef,
    cv, sv, rn, dp, sn, zr, zd, za, mine, theirs, stats,
    in_sem, t_send, t_recv, z_send, z_recv, s_send, s_recv, gate,
):
    L = rv.shape[0]
    N = T * S
    F = L // 2 - 1
    others = [k for k in range(L) if k != F]
    t, s = lax.axis_index("tm"), lax.axis_index("space")
    me = t * S + s
    earlier, later = t > 0, t < T - 1
    lower, upper = s > 0, s < S - 1
    beyond = ((earlier, {"tm": t - 1}), (later, {"tm": t + 1}), (lower, {"space": s - 1}), (upper, {"space": s + 1}))
    count = sum(jnp.where(when, 1, 0) for when, _ in beyond)

    loads = [
        pltpu.make_async_copy(src, dst, in_sem.at[i])
        for i, (src, dst) in enumerate(((d_in, dv), (c_in, cv), (r_in, rv), (x_in, xv)))
    ]
    for load in loads:
        load.start()

    def greet(sem):
        for when, place in beyond:
            @pl.when(when)
            def _():
                pl.semaphore_signal(sem, inc=1, device_id=place, device_id_type=MESH)

    barrier = pltpu.get_barrier_semaphore()
    greet(barrier)

    @pl.when(jnp.logical_not(earlier))
    def _():
        dp[...] = jnp.zeros_like(dp)

    @pl.when(jnp.logical_not(later))
    def _():
        rn[...] = jnp.zeros_like(rn)
        sn[...] = jnp.zeros_like(sn)

    @pl.when(jnp.logical_not(lower))
    def _():
        for z in (zr, zd, za):
            z[0] = jnp.zeros(z.shape[1:], z.dtype)

    @pl.when(jnp.logical_not(upper))
    def _():
        for z in (zr, zd, za):
            z[1] = jnp.zeros(z.shape[1:], z.dtype)

    pl.semaphore_wait(barrier, count)

    rounds = T + S - 3
    share = -(-rounds // 5)
    done = [0]

    def pass_on():
        for _ in range(min(share, rounds - done[0])):
            greet(gate.at[done[0]])
            pl.semaphore_wait(gate.at[done[0]], count)
            done[0] += 1

    def step_copy(i, src, dst, k, to):
        return pltpu.make_async_remote_copy(
            src_ref=src.at[k], dst_ref=dst.at[k], send_sem=t_send.at[i, k], recv_sem=t_recv.at[i, k],
            device_id={"tm": to}, device_id_type=MESH)

    def layer_copy(i, src, dst, up):
        return pltpu.make_async_remote_copy(
            src_ref=src.at[L - 1 if up else 0], dst_ref=dst.at[0 if up else 1],
            send_sem=z_send.at[i, 0 if up else 1], recv_sem=z_recv.at[i, 0 if up else 1],
            device_id={"space": s + 1 if up else s - 1}, device_id_type=MESH)

    d_step = [step_copy(0, d_in, dp, k, t + 1) for k in range(L)]
    r_step = [step_copy(1, r_in, rn, k, t - 1) for k in range(L)]
    s_step = [step_copy(2, sv, sn, k, t - 1) for k in range(L)]
    f_step = [step_copy(3, mine, theirs, i, t + 1) for i in range(2)]
    d_up, d_down = layer_copy(0, d_in, zd, True), layer_copy(0, d_in, zd, False)
    r_up, r_down = layer_copy(1, r_in, zr, True), layer_copy(1, r_in, zr, False)
    a_up, a_down = layer_copy(2, av, za, True), layer_copy(2, av, za, False)

    def go(when, *copies):
        @pl.when(when)
        def _():
            for copy in copies:
                copy.start()

    def arrive(when, *copies):
        @pl.when(when)
        def _():
            for copy in copies:
                copy.wait_recv()

    go(upper, d_up)
    go(lower, d_down)
    go(later, *d_step)
    go(earlier, *[r_step[k] for k in others])
    go(upper, r_up)
    go(lower, r_down)

    for load in loads:
        load.wait()
    middle = [k for k in range(1, L - 1)]
    for k in middle:
        sv[k] = spatial(dv, zd, cv[k], k)
        if k != F:
            go(earlier, s_step[k])
    arrive(lower, d_up)
    arrive(upper, d_down)
    for k in (0, L - 1):
        sv[k] = spatial(dv, zd, cv[k], k)
        if k != F:
            go(earlier, s_step[k])
    pass_on()
    for k in middle:
        gv[k] = spatial(rv, zr, cv[k], k)
    mine[0] = gv[F]
    go(later, f_step[0])
    arrive(lower, r_up)
    arrive(upper, r_down)
    for k in (0, L - 1):
        gv[k] = spatial(rv, zr, cv[k], k)
    pass_on()

    aa = jnp.zeros((1, cv.shape[2]), jnp.float32)
    for k in range(L):
        arrive(earlier, d_step[k])
        image = sv[k] - cv[k] * dp[k]
        av[k] = image
        aa = aa + folded(image * image)
        if k == 0:
            go(lower, a_down)
        if k == F + 1:
            mine[1] = spatial(av, za, cv[F], F)
            go(later, f_step[1])
        if k == L - 1:
            go(upper, a_up)
        if k < 3:
            pass_on()
    go(earlier, r_step[F], s_step[F])

    gg = jnp.zeros((1, cv.shape[2]), jnp.float32)
    for k in others:
        arrive(later, r_step[k])
        gradient = gv[k] - cv[k] * rn[k]
        gv[k] = gradient
        gg = gg + folded(gradient * gradient)

    has_next = jnp.where(later, 1.0, 0.0)
    gw = jnp.zeros((1, cv.shape[2]), jnp.float32)
    ww = jnp.zeros((1, cv.shape[2]), jnp.float32)
    for k in others:
        if k not in (0, L - 1):
            wv[k] = spatial(av, za, cv[k], k)
    arrive(lower, a_up)
    arrive(upper, a_down)
    for k in (0, L - 1):
        wv[k] = spatial(av, za, cv[k], k)
    for k in others:
        arrive(later, s_step[k])
        change = wv[k] - cv[k] * (has_next * (sn[k] - cv[k] * dv[k]))
        wv[k] = change
        gw = gw + folded(gv[k] * change)
        ww = ww + folded(change * change)

    stats[me] = jnp.concatenate([gg, aa, gw, ww, gg, aa, gw, ww], axis=0)

    def add(gradient, change):
        square = folded(gradient * gradient)
        stats[me] += jnp.concatenate(
            [square, jnp.zeros_like(square), folded(gradient * change), folded(change * change)] * 2, axis=0)

    @pl.when(earlier)
    def _():
        for copy in f_step:
            copy.wait_recv()
        add(theirs[0] - cv[F] * rv[F], theirs[1] - cv[F] * av[F])

    @pl.when(jnp.logical_not(later))
    def _():
        add(mine[0], mine[1])

    def peer(o):
        other = lax.rem(me + o, N)
        return {"tm": lax.div(other, S), "space": lax.rem(other, S)}

    def each_peer(do):
        if N <= 16:
            for o in sorted(range(1, N), key=lambda o: -min(o, N - o)):
                do(o)
        else:
            def body(o, carry):
                do(o)
                return carry
            lax.fori_loop(1, N, body, 0)

    def stat_copy(o):
        return pltpu.make_async_remote_copy(
            src_ref=stats.at[me], dst_ref=stats.at[me], send_sem=s_send.at[o], recv_sem=s_recv.at[me],
            device_id=peer(o), device_id_type=MESH)

    def stat_wait(o):
        other = lax.rem(me + o, N)
        pltpu.make_async_remote_copy(
            src_ref=stats.at[other], dst_ref=stats.at[other], send_sem=s_send.at[o], recv_sem=s_recv.at[other],
            device_id=peer(o), device_id_type=MESH).wait_recv()

    each_peer(lambda o: stat_copy(o).start())

    arrive(later, r_step[F], s_step[F])
    gv[F] = mine[0] - cv[F] * rn[F]
    wv[F] = mine[1] - cv[F] * (has_next * (sn[F] - cv[F] * dv[F]))

    def sent(when, *copies):
        @pl.when(when)
        def _():
            for copy in copies:
                copy.wait_send()

    sent(later, *d_step, *f_step)
    sent(earlier, *r_step, *s_step)
    sent(upper, d_up, r_up, a_up)
    sent(lower, d_down, r_down, a_down)
    each_peer(stat_wait)

    whole = jnp.sum(jnp.sum(stats[...], axis=0), axis=1, keepdims=True)
    whole = jnp.broadcast_to(whole, (8, coef.shape[1]))
    grad_norm, image_norm, cross, change_norm = (whole[i:i + 1] for i in range(4))
    step_size = grad_norm / image_norm
    new_norm = grad_norm + step_size * (step_size * change_norm - 2.0 * cross)
    ratio = new_norm / grad_norm
    coef[...] = jnp.concatenate([step_size, ratio] * 4, axis=0)
    each_peer(lambda o: stat_copy(o).wait_send())


def finish(x, r, d, a, g, w, coef, x_out, r_out, d_out, xs, rs, ds, sem):
    step_size, ratio = coef[0:1], coef[1:2]
    writes = []
    for k in range(x.shape[0]):
        xs[k] = x[k] + step_size * d[k]
        rs[k] = r[k] - step_size * a[k]
        ds[k] = g[k] - step_size * w[k] + ratio * d[k]
        for i, (src, dst) in enumerate(((xs, x_out), (rs, r_out), (ds, d_out))):
            write = pltpu.make_async_copy(src.at[k], dst.at[k], sem.at[i, k])
            write.start()
            writes.append(write)
    for write in writes:
        write.wait()


def local(T, S, solution, residual, direction, capacity):
    L, X, Y = capacity.shape
    field = jax.ShapeDtypeStruct((L, X, Y), jnp.float32)
    whole = pltpu.VMEM((L, X, Y), jnp.float32)
    halo = pltpu.VMEM((2, X, Y), jnp.float32)
    near, far = pl.BlockSpec(memory_space=pltpu.VMEM), pl.BlockSpec(memory_space=pltpu.HBM)
    kept = pl.pallas_call(
        functools.partial(exchange, T, S),
        out_shape=(field,) * 6 + (jax.ShapeDtypeStruct((8, Y), jnp.float32),),
        in_specs=[far] * 4,
        out_specs=(near,) * 7,
        scratch_shapes=[whole] * 5 + [halo] * 5 + [
            pltpu.VMEM((T * S, 8, Y), jnp.float32),
            pltpu.SemaphoreType.DMA((4,)),
            pltpu.SemaphoreType.DMA((4, L)),
            pltpu.SemaphoreType.DMA((4, L)),
            pltpu.SemaphoreType.DMA((3, 2)),
            pltpu.SemaphoreType.DMA((3, 2)),
            pltpu.SemaphoreType.DMA((T * S,)),
            pltpu.SemaphoreType.DMA((T * S,)),
            pltpu.SemaphoreType.REGULAR((T + S - 3,)),
        ],
        compiler_params=pltpu.CompilerParams(
            collective_id=0, has_side_effects=True, vmem_limit_bytes=53568 * 1024),
    )(solution[0], residual[0], direction[0], capacity)
    outs = pl.pallas_call(
        finish,
        out_shape=(field,) * 3,
        in_specs=[near] * 7,
        out_specs=(far,) * 3,
        scratch_shapes=[whole] * 3 + [pltpu.SemaphoreType.DMA((3, L))],
        compiler_params=pltpu.CompilerParams(vmem_limit_bytes=16 * 1024 * 1024),
    )(*kept)
    return tuple(out[None] for out in outs)


def solution(mesh):
    field = P(("groups", "tm"), "space", None, None)
    return jax.shard_map(
        functools.partial(local, mesh.shape["tm"], mesh.shape["space"]),
        mesh=mesh,
        in_specs=(field, field, field, P(("groups", "space"), None, None)),
        out_specs=(field, field, field),
        check_vma=False,
    )
```

time: 24.5 us -> 23.7 us (0.967)
  Pallas kernels: 23.7 us -> 22.9 us
    pallas_call x1, Pallas kernels: 22.7 us -> 21.9 us  [local(): pl.pallas_call(functools.partial(exchange, T, S), out_shape=(field,) * 6...]
where the time goes in v3:
time: 23.7 us; the launch traced here: 23.6 us
  Pallas kernels  22.9 us (97%)
  between operations  0.64 us (3%)
    pallas_call x1, Pallas kernels, local(): pl.pallas_call(functools.partial(exchange, T, S), out_shape=(field,) * 6...  21.9 us
    pallas_call x1, Pallas kernels, local(): pl.pallas_call(finish, out_shape=(field,) * 3, in_specs=[near] * 7, out_s...  0.98 us

profile of v3, /device:TPU:0, one launch (start us, length us, event | category | flops | bytes accessed | tf_op | source)
XLA Modules:
  0.0 23.6 jit_solution(5426851737663153935)
XLA Ops:
  0.6 21.9 %shard_map.67 = (f32[4,128,128]{2,1,0:T(8,128)S(1)}, f32[4,128,128]{2,1,0:T(8,128)S(1)}, f32[4,128,128]{2,1,0:T(8,128)S(1)}, f32[4,128,128]{2,1,0:T(8,128)S(1)},...) custom-call(f32[4,128,128]{2,1,0:T(8,128)} %bitcast.6, f32[4,128,128]{2,1,0:T(8,128)} %bitcast.7, ...), custom_call_target="tpu_custom_call" | custom-call | tf_op jit(solution)/shard_map/pallas_call | solution.py:293
  22.6 1.0 %shard_map.68 = (f32[4,128,128]{2,1,0:T(8,128)}, f32[4,128,128]{2,1,0:T(8,128)}, f32[4,128,128]{2,1,0:T(8,128)}) custom-call(f32[4,128,128]{2,1,0:T(8,128)S(1)} %get-tuple-element.13.x, f32[4,128,128]{2,1,0:T(8,128)S(1)} %get-tuple-element.14.r, f32[4,128,128]{2,1,0:T(8,128)S(1)} %get-tuple-element.15.d, f32[4,128,128]{2,1,0:T(8,128)S(1)} %get-tuple-element.16.a, ...), custom_call_target="tpu_custom_call" | custom-call | tf_op jit(solution)/shard_map/pallas_call | solution.py:312

commit v4 on v3

--- a/solution.py
+++ b/solution.py
@@ -87,14 +87,17 @@
     pl.semaphore_wait(barrier, count)
 
     rounds = T + S - 3
-    share = -(-rounds // 5)
+    share = -(-(rounds - 1) // 4)
     done = [0]
 
-    def pass_on():
-        for _ in range(min(share, rounds - done[0])):
-            greet(gate.at[done[0]])
+    def pass_on(limit=rounds):
+        for _ in range(min(limit, rounds - done[0])):
             pl.semaphore_wait(gate.at[done[0]], count)
             done[0] += 1
+            if done[0] < rounds:
+                greet(gate.at[done[0]])
+
+    greet(gate.at[0])
 
     def step_copy(i, src, dst, k, to):
         return pltpu.make_async_remote_copy(
@@ -147,7 +150,7 @@
         sv[k] = spatial(dv, zd, cv[k], k)
         if k != F:
             go(earlier, s_step[k])
-    pass_on()
+    pass_on(share)
     for k in middle:
         gv[k] = spatial(rv, zr, cv[k], k)
     mine[0] = gv[F]
@@ -156,7 +159,7 @@
     arrive(upper, r_down)
     for k in (0, L - 1):
         gv[k] = spatial(rv, zr, cv[k], k)
-    pass_on()
+    pass_on(share)
 
     aa = jnp.zeros((1, cv.shape[2]), jnp.float32)
     for k in range(L):
@@ -171,9 +174,9 @@
             go(later, f_step[1])
         if k == L - 1:
             go(upper, a_up)
-        if k < 3:
-            pass_on()
-    go(earlier, r_step[F], s_step[F])
+        if k < 2:
+            pass_on(share)
+    go(earlier, r_step[F])
 
     gg = jnp.zeros((1, cv.shape[2]), jnp.float32)
     for k in others:
@@ -241,7 +244,9 @@
             src_ref=stats.at[other], dst_ref=stats.at[other], send_sem=s_send.at[o], recv_sem=s_recv.at[other],
             device_id=peer(o), device_id_type=MESH).wait_recv()
 
+    pass_on()
     each_peer(lambda o: stat_copy(o).start())
+    go(earlier, s_step[F])
 
     arrive(later, r_step[F], s_step[F])
     gv[F] = mine[0] - cv[F] * rn[F]

time: 23.7 us -> 22.2 us (0.937)
  Pallas kernels: 22.9 us -> 21.4 us
    pallas_call x1, Pallas kernels: 21.9 us -> 20.4 us  [local(): pl.pallas_call(functools.partial(exchange, T, S), out_shape=(field,) * 6...]
where the time goes in v4:
time: 22.2 us; the launch traced here: 22.1 us
  Pallas kernels  21.4 us (96%)
  between operations  0.64 us (3%)
    pallas_call x1, Pallas kernels, local(): pl.pallas_call(functools.partial(exchange, T, S), out_shape=(field,) * 6...  20.4 us
    pallas_call x1, Pallas kernels, local(): pl.pallas_call(finish, out_shape=(field,) * 3, in_specs=[near] * 7, out_s...  0.98 us

profile of v4, /device:TPU:0, one launch (start us, length us, event | category | flops | bytes accessed | tf_op | source)
XLA Modules:
  0.0 22.1 jit_solution(13513082852631079162)
XLA Ops:
  0.6 20.4 %shard_map.67 = (f32[4,128,128]{2,1,0:T(8,128)S(1)}, f32[4,128,128]{2,1,0:T(8,128)S(1)}, f32[4,128,128]{2,1,0:T(8,128)S(1)}, f32[4,128,128]{2,1,0:T(8,128)S(1)},...) custom-call(f32[4,128,128]{2,1,0:T(8,128)} %bitcast.6, f32[4,128,128]{2,1,0:T(8,128)} %bitcast.7, ...), custom_call_target="tpu_custom_call" | custom-call | tf_op jit(solution)/shard_map/pallas_call | solution.py:298
  21.1 1.0 %shard_map.68 = (f32[4,128,128]{2,1,0:T(8,128)}, f32[4,128,128]{2,1,0:T(8,128)}, f32[4,128,128]{2,1,0:T(8,128)}) custom-call(f32[4,128,128]{2,1,0:T(8,128)S(1)} %get-tuple-element.13.x, f32[4,128,128]{2,1,0:T(8,128)S(1)} %get-tuple-element.14.r, f32[4,128,128]{2,1,0:T(8,128)S(1)} %get-tuple-element.15.d, f32[4,128,128]{2,1,0:T(8,128)S(1)} %get-tuple-element.16.a, ...), custom_call_target="tpu_custom_call" | custom-call | tf_op jit(solution)/shard_map/pallas_call | solution.py:317

commit v5 on v4

--- a/solution.py
+++ b/solution.py
@@ -62,6 +62,23 @@
             def _():
                 pl.semaphore_signal(sem, inc=1, device_id=place, device_id_type=MESH)
 
+    def turned(i, by, n):
+        return jnp.where(i + by >= n, i + by - n, i + by)
+
+    def shift(o):
+        if isinstance(o, int):
+            return turned(t, o // S, T), turned(s, o % S, S)
+        return turned(t, lax.div(o, S), T), turned(s, lax.rem(o, S), S)
+
+    known = {o: shift(o) for o in range(1, N)} if N <= 16 else {}
+
+    def place_of(o):
+        return known[o] if isinstance(o, int) else shift(o)
+
+    def peer(o):
+        other_t, other_s = place_of(o)
+        return {"tm": other_t, "space": other_s}
+
     barrier = pltpu.get_barrier_semaphore()
     greet(barrier)
 
@@ -132,10 +149,10 @@
 
     go(upper, d_up)
     go(lower, d_down)
+    go(upper, r_up)
+    go(lower, r_down)
     go(later, *d_step)
     go(earlier, *[r_step[k] for k in others])
-    go(upper, r_up)
-    go(lower, r_down)
 
     for load in loads:
         load.wait()
@@ -188,26 +205,29 @@
     has_next = jnp.where(later, 1.0, 0.0)
     gw = jnp.zeros((1, cv.shape[2]), jnp.float32)
     ww = jnp.zeros((1, cv.shape[2]), jnp.float32)
+    nothing = jnp.zeros(cv.shape[1:], jnp.float32)
+    wv[0] = (6.0 + cv[0]) * av[0] - beside(av[0], nothing, av[1])
     for k in others:
         if k not in (0, L - 1):
             wv[k] = spatial(av, za, cv[k], k)
-    arrive(lower, a_up)
     arrive(upper, a_down)
-    for k in (0, L - 1):
-        wv[k] = spatial(av, za, cv[k], k)
-    for k in others:
+    wv[L - 1] = spatial(av, za, cv[L - 1], L - 1)
+    for k in others[1:] + others[:1]:
         arrive(later, s_step[k])
         change = wv[k] - cv[k] * (has_next * (sn[k] - cv[k] * dv[k]))
+        if k == 0:
+            arrive(lower, a_up)
+            change = change - za[0]
         wv[k] = change
         gw = gw + folded(gv[k] * change)
         ww = ww + folded(change * change)
 
-    stats[me] = jnp.concatenate([gg, aa, gw, ww, gg, aa, gw, ww], axis=0)
+    stats[me] = jnp.concatenate([gg, aa, gw, ww], axis=0)
 
     def add(gradient, change):
         square = folded(gradient * gradient)
         stats[me] += jnp.concatenate(
-            [square, jnp.zeros_like(square), folded(gradient * change), folded(change * change)] * 2, axis=0)
+            [square, jnp.zeros_like(square), folded(gradient * change), folded(change * change)], axis=0)
 
     @pl.when(earlier)
     def _():
@@ -218,10 +238,6 @@
     @pl.when(jnp.logical_not(later))
     def _():
         add(mine[0], mine[1])
-
-    def peer(o):
-        other = lax.rem(me + o, N)
-        return {"tm": lax.div(other, S), "space": lax.rem(other, S)}
 
     def each_peer(do):
         if N <= 16:
@@ -239,7 +255,8 @@
             device_id=peer(o), device_id_type=MESH)
 
     def stat_wait(o):
-        other = lax.rem(me + o, N)
+        other_t, other_s = place_of(o)
+        other = other_t * S + other_s
         pltpu.make_async_remote_copy(
             src_ref=stats.at[other], dst_ref=stats.at[other], send_sem=s_send.at[o], recv_sem=s_recv.at[other],
             device_id=peer(o), device_id_type=MESH).wait_recv()
@@ -265,7 +282,7 @@
     each_peer(stat_wait)
 
     whole = jnp.sum(jnp.sum(stats[...], axis=0), axis=1, keepdims=True)
-    whole = jnp.broadcast_to(whole, (8, coef.shape[1]))
+    whole = jnp.broadcast_to(whole, (4, coef.shape[1]))
     grad_norm, image_norm, cross, change_norm = (whole[i:i + 1] for i in range(4))
     step_size = grad_norm / image_norm
     new_norm = grad_norm + step_size * (step_size * change_norm - 2.0 * cross)
@@ -301,7 +318,7 @@
         in_specs=[far] * 4,
         out_specs=(near,) * 7,
         scratch_shapes=[whole] * 5 + [halo] * 5 + [
-            pltpu.VMEM((T * S, 8, Y), jnp.float32),
+            pltpu.VMEM((T * S, 4, Y), jnp.float32),
             pltpu.SemaphoreType.DMA((4,)),
             pltpu.SemaphoreType.DMA((4, L)),
             pltpu.SemaphoreType.DMA((4, L)),

time: 22.2 us -> 21.7 us (0.977)
  Pallas kernels: 21.4 us -> 20.9 us
    pallas_call x1, Pallas kernels: 20.4 us -> 20 us  [local(): pl.pallas_call(functools.partial(exchange, T, S), out_shape=(field,) * 6...]
where the time goes in v5:
time: 21.7 us; the launch traced here: 21.6 us
  Pallas kernels  20.9 us (96%)
  between operations  0.64 us (3%)
    pallas_call x1, Pallas kernels, local(): pl.pallas_call(functools.partial(exchange, T, S), out_shape=(field,) * 6...  20 us
    pallas_call x1, Pallas kernels, local(): pl.pallas_call(finish, out_shape=(field,) * 3, in_specs=[near] * 7, out_s...  0.98 us

profile of v5, /device:TPU:0, one launch (start us, length us, event | category | flops | bytes accessed | tf_op | source)
XLA Modules:
  0.0 21.6 jit_solution(15940948137765974229)
XLA Ops:
  0.6 20.0 %shard_map.67 = (f32[4,128,128]{2,1,0:T(8,128)S(1)}, f32[4,128,128]{2,1,0:T(8,128)S(1)}, f32[4,128,128]{2,1,0:T(8,128)S(1)}, f32[4,128,128]{2,1,0:T(8,128)S(1)},...) custom-call(f32[4,128,128]{2,1,0:T(8,128)} %bitcast.6, f32[4,128,128]{2,1,0:T(8,128)} %bitcast.7, ...), custom_call_target="tpu_custom_call" | custom-call | tf_op jit(solution)/shard_map/pallas_call | solution.py:315
  20.6 1.0 %shard_map.68 = (f32[4,128,128]{2,1,0:T(8,128)}, f32[4,128,128]{2,1,0:T(8,128)}, f32[4,128,128]{2,1,0:T(8,128)}) custom-call(f32[4,128,128]{2,1,0:T(8,128)S(1)} %get-tuple-element.13.x, f32[4,128,128]{2,1,0:T(8,128)S(1)} %get-tuple-element.14.r, f32[4,128,128]{2,1,0:T(8,128)S(1)} %get-tuple-element.15.d, f32[4,128,128]{2,1,0:T(8,128)S(1)} %get-tuple-element.16.a, ...), custom_call_target="tpu_custom_call" | custom-call | tf_op jit(solution)/shard_map/pallas_call | solution.py:334

commit v6 on v5

--- a/solution.py
+++ b/solution.py
@@ -212,8 +212,27 @@
             wv[k] = spatial(av, za, cv[k], k)
     arrive(upper, a_down)
     wv[L - 1] = spatial(av, za, cv[L - 1], L - 1)
+    def add(gradient, change):
+        square = folded(gradient * gradient)
+        stats[me] += jnp.concatenate(
+            [square, jnp.zeros_like(square), folded(gradient * change), folded(change * change)], axis=0)
+
     for k in others[1:] + others[:1]:
         arrive(later, s_step[k])
+        if k == 0:
+            stats[me] = jnp.concatenate([gg, aa, gw, ww], axis=0)
+
+            @pl.when(earlier)
+            def _():
+                for copy in f_step:
+                    copy.wait_recv()
+                add(theirs[0] - cv[F] * rv[F], theirs[1] - cv[F] * av[F])
+
+            @pl.when(jnp.logical_not(later))
+            def _():
+                add(mine[0], mine[1])
+
+            gw, ww = jnp.zeros_like(gw), jnp.zeros_like(ww)
         change = wv[k] - cv[k] * (has_next * (sn[k] - cv[k] * dv[k]))
         if k == 0:
             arrive(lower, a_up)
@@ -222,22 +241,8 @@
         gw = gw + folded(gv[k] * change)
         ww = ww + folded(change * change)
 
-    stats[me] = jnp.concatenate([gg, aa, gw, ww], axis=0)
-
-    def add(gradient, change):
-        square = folded(gradient * gradient)
-        stats[me] += jnp.concatenate(
-            [square, jnp.zeros_like(square), folded(gradient * change), folded(change * change)], axis=0)
-
-    @pl.when(earlier)
-    def _():
-        for copy in f_step:
-            copy.wait_recv()
-        add(theirs[0] - cv[F] * rv[F], theirs[1] - cv[F] * av[F])
-
-    @pl.when(jnp.logical_not(later))
-    def _():
-        add(mine[0], mine[1])
+    nil = jnp.zeros_like(gw)
+    stats[me] += jnp.concatenate([nil, nil, gw, ww], axis=0)
 
     def each_peer(do):
         if N <= 16:

time: 21.7 us -> 21.7 us (level)
  no operation moved by 1% of the time
where the time goes in v6:
time: 21.7 us; the launch traced here: 21.6 us
  Pallas kernels  20.9 us (96%)
  between operations  0.64 us (3%)
    pallas_call x1, Pallas kernels, local(): pl.pallas_call(functools.partial(exchange, T, S), out_shape=(field,) * 6...  20 us
    pallas_call x1, Pallas kernels, local(): pl.pallas_call(finish, out_shape=(field,) * 3, in_specs=[near] * 7, out_s...  0.98 us

profile of v6, /device:TPU:0, one launch (start us, length us, event | category | flops | bytes accessed | tf_op | source)
XLA Modules:
  0.0 21.6 jit_solution(681063774933150222)
XLA Ops:
  0.6 20.0 %shard_map.67 = (f32[4,128,128]{2,1,0:T(8,128)S(1)}, f32[4,128,128]{2,1,0:T(8,128)S(1)}, f32[4,128,128]{2,1,0:T(8,128)S(1)}, f32[4,128,128]{2,1,0:T(8,128)S(1)},...) custom-call(f32[4,128,128]{2,1,0:T(8,128)} %bitcast.6, f32[4,128,128]{2,1,0:T(8,128)} %bitcast.7, ...), custom_call_target="tpu_custom_call" | custom-call | tf_op jit(solution)/shard_map/pallas_call | solution.py:320
  20.6 1.0 %shard_map.68 = (f32[4,128,128]{2,1,0:T(8,128)}, f32[4,128,128]{2,1,0:T(8,128)}, f32[4,128,128]{2,1,0:T(8,128)}) custom-call(f32[4,128,128]{2,1,0:T(8,128)S(1)} %get-tuple-element.13.x, f32[4,128,128]{2,1,0:T(8,128)S(1)} %get-tuple-element.14.r, f32[4,128,128]{2,1,0:T(8,128)S(1)} %get-tuple-element.15.d, f32[4,128,128]{2,1,0:T(8,128)S(1)} %get-tuple-element.16.a, ...), custom_call_target="tpu_custom_call" | custom-call | tf_op jit(solution)/shard_map/pallas_call | solution.py:339
